TPU v7x, 32 devices: a whole 2x2x4 slice. The times are simulated.
32 devices in a mesh: ctx: 2 (over y), exp: 16 (over z, x, core).
Axes of the slice: x: 2, y: 2, z: 4, core: 2. Of those that a mesh axis runs over, the one named last changes fastest.
Arguments:
- inputs: bfloat16 [1536, 1024], P('exp', 'ctx'), may hold values from -6 to 6
- pre_act: bfloat16 [1536, 1024], P('exp', 'ctx'), may hold values from -6 to 6
- grad_out: bfloat16 [1536, 1024], P('exp', 'ctx'), may hold values from -6 to 6
- conv_weight: bfloat16 [5, 1536, 1536], P(None, 'exp', 'ctx'), may hold values from -0.0625 to 0.0625
- expert_ids: int32 [1024, 2], P('ctx'), may hold values from 0 to 15, as said below
- gate_values: float32 [1024, 2], P('ctx'), may hold values from 0.1 to 0.9
- expert_in: bfloat16 [16, 1536, 3072], P('exp', None, 'ctx'), may hold values from -0.15625 to 0.15625
- expert_out: bfloat16 [16, 3072, 1536], P('exp', 'ctx'), may hold values from -0.109375 to 0.109375
Outputs:
- grad_inputs: bfloat16 [1536, 1024], P('exp', 'ctx')
- grad_conv: float32 [5, 1536, 1536], P(None, 'exp', 'ctx')
- grad_expert_in: bfloat16 [16, 1536, 3072], P('exp', None, 'ctx')
- grad_expert_out: bfloat16 [16, 3072, 1536], P('exp', 'ctx')
Inputs may be any that keep to these rules, and one draw needn't show every extreme that they name: `expert_ids`: the 2 ids of a bin differ. In each aligned block of 512 bins (the bins of one index of ctx) no expert is named more than 128 times, and one expert, the same in every block, is named exactly 128 times in each block.
All inputs are finite; a program needn't handle non-finite values.
Results may differ from a plain program's by a relative error of at most 0.009.
Values may be sent and summed in bfloat16 or wider, within the bound.
A program may use at most 128 MiB of HBM per device.

v0:
```python
import jax
import jax.numpy as jnp
from jax import lax
from jax.sharding import PartitionSpec as P


def with_halo(cells, sides, width):
    for axis, dim in sides:
        count = lax.axis_size(axis)
        ends = count - 1
        head = lax.slice_in_dim(cells, 0, width, axis=dim)
        tail = lax.slice_in_dim(cells, cells.shape[dim] - width, cells.shape[dim], axis=dim)
        cells = jnp.concatenate(
            [
                lax.ppermute(tail, axis, [(i, (i + 1) % count) for i in range(ends)]),
                cells,
                lax.ppermute(head, axis, [((i + 1) % count, i) for i in range(ends)]),
            ],
            axis=dim,
        )
    return cells


def gelu_value(values):
    factor = 0.7978845608028654
    return 0.5 * values * (1.0 + jnp.tanh(factor * (values + 0.044715 * values * values * values)))


def gelu_slope(values):
    factor = 0.7978845608028654
    tangent = jnp.tanh(factor * (values + 0.044715 * values * values * values))
    return 0.5 * (1.0 + tangent) + 0.5 * values * (1.0 - tangent * tangent) * factor * (
        1.0 + 0.134145 * values * values
    )


def turned(left, right, dims):
    return lax.dot_general(
        left.astype(jnp.float32),
        right.astype(jnp.float32),
        (dims, ((), ())),
        preferred_element_type=jnp.float32,
    )


def expert_pass(w_first, w_second, rows_in, rows_grad):
    hidden = turned(w_first, rows_in, ((0,), (0,)))
    squashed = gelu_value(hidden).astype(jnp.bfloat16)
    grad_second = turned(squashed, rows_grad, ((1,), (1,)))
    grad_hidden = jnp.dot(w_second, rows_grad, preferred_element_type=jnp.float32)
    grad_pre = (grad_hidden * gelu_slope(hidden)).astype(jnp.bfloat16)
    grad_first = turned(rows_in, grad_pre, ((1,), (1,)))
    grad_rows = jnp.dot(w_first, grad_pre, preferred_element_type=jnp.float32)
    return (grad_first, grad_second, grad_rows)


def local(inputs, pre_act, grad_out, conv_weight, expert_ids, gate_values, expert_in, expert_out):
    channels, bins_local = inputs.shape
    experts = lax.axis_size("exp")
    groups = lax.axis_size("ctx")
    capacity = 4 * bins_local // experts
    model_width = channels * experts
    kernel = conv_weight.shape[0]
    margin = kernel // 2
    pre_float = pre_act.astype(jnp.float32)
    activated = (inputs.astype(jnp.float32) + gelu_value(pre_float)).astype(jnp.bfloat16)
    grad_float = grad_out.astype(jnp.float32)
    flat_ids = expert_ids.reshape(-1)
    onehot = (flat_ids[:, None] == jnp.arange(experts, dtype=jnp.int32)[None, :]).astype(jnp.int32)
    slot_index = jnp.sum(onehot * jnp.cumsum(onehot, axis=0), axis=1) - 1
    targets = flat_ids * capacity + slot_index
    owners = jnp.arange(flat_ids.shape[0], dtype=jnp.int32) // expert_ids.shape[1]
    row_table = jnp.full((experts * capacity,), bins_local, jnp.int32).at[targets].set(owners)
    gate_table = (
        jnp.zeros((experts * capacity,), jnp.float32).at[targets].set(gate_values.reshape(-1))
    )
    act_pad = jnp.concatenate([activated, jnp.zeros((channels, 1), jnp.bfloat16)], axis=1)
    grad_pad = jnp.concatenate([grad_float, jnp.zeros((channels, 1), jnp.float32)], axis=1)
    send_rows = act_pad[:, row_table].reshape(channels, experts, capacity)
    send_grad = (
        (grad_pad[:, row_table] * gate_table[None, :])
        .astype(jnp.bfloat16)
        .reshape(channels, experts, capacity)
    )
    weight_first = expert_in[0]
    weight_second = expert_out[0]
    total_rows = groups * capacity
    copied = (
        lax.all_gather(send_rows, "ctx", axis=2, tiled=True),
        lax.all_gather(send_grad, "ctx", axis=2, tiled=True),
    )
    arrived = (
        lax.all_to_all(copied[0], "exp", split_axis=1, concat_axis=0, tiled=True),
        lax.all_to_all(copied[1], "exp", split_axis=1, concat_axis=0, tiled=True),
    )
    part_in, part_out, part_rows = expert_pass(
        weight_first, weight_second, arrived[0][:, 0, :], arrived[1][:, 0, :]
    )
    rows_back = part_rows
    sum_first, sum_second, rows_back = (part_in, part_out, rows_back)
    moved_back = lax.all_to_all(
        rows_back.reshape(model_width, 1, total_rows),
        "exp",
        split_axis=0,
        concat_axis=1,
        tiled=True,
    )
    returned = lax.psum_scatter(moved_back, "ctx", scatter_dimension=2, tiled=True).astype(
        jnp.bfloat16
    )
    back_flat = returned.reshape(channels, experts * capacity).astype(jnp.float32)
    per_bin = targets.reshape(bins_local, -1)
    grad_total = grad_float
    for column in range(per_bin.shape[1]):
        grad_total = grad_total + back_flat[:, per_bin[:, column]]
    grad_pre_conv = (grad_total * gelu_slope(pre_float)).astype(jnp.bfloat16)
    full_weight = lax.all_gather(conv_weight, "ctx", axis=2, tiled=True)
    rim_inputs = with_halo(inputs, (("ctx", 1),), margin)
    gathered = lax.all_gather(grad_pre_conv, "exp", axis=0, tiled=True)
    rim_grad = with_halo(gathered, (("ctx", 1),), margin)
    conv_back = jnp.zeros((channels, bins_local), jnp.float32)
    tap_grads = []
    for offset in range(kernel):
        lower = 2 * margin - offset
        weight_cols = full_weight[offset]
        conv_back = conv_back + jnp.dot(
            weight_cols, rim_grad[:, lower : lower + bins_local], preferred_element_type=jnp.float32
        )
        tap_grads.append(
            turned(
                rim_inputs[:, offset : offset + bins_local],
                rim_grad[:, margin : margin + bins_local],
                ((1,), (1,)),
            )
        )
    conv_grad = jnp.stack(tap_grads)
    conv_back, conv_grad = (conv_back, conv_grad)
    grad_inputs = (grad_total + conv_back).astype(jnp.bfloat16)
    grad_conv = lax.psum_scatter(
        conv_grad.astype(jnp.bfloat16), "ctx", scatter_dimension=2, tiled=True
    ).astype(jnp.float32)
    return (
        grad_inputs,
        grad_conv,
        sum_first.astype(jnp.bfloat16)[None],
        sum_second.astype(jnp.bfloat16)[None],
    )


def solution(mesh):
    placed = (
        P("exp", "ctx"),
        P("exp", "ctx"),
        P("exp", "ctx"),
        P(None, "exp", "ctx"),
        P("ctx", None),
        P("ctx", None),
        P("exp", None, "ctx"),
        P("exp", "ctx", None),
    )
    return jax.shard_map(
        local,
        mesh=mesh,
        in_specs=placed,
        out_specs=(
            P("exp", "ctx"),
            P(None, "exp", "ctx"),
            P("exp", None, "ctx"),
            P("exp", "ctx", None),
        ),
        check_vma=False,
    )
```

profile of v0, /device:TPU:0, one launch (start us, length us, event | category | flops | bytes accessed | tf_op | source)
XLA Modules:
  0.0 288.9 jit_solution(6828851017552488800)
XLA Ops:
  7.2 0.9 copy.47
  8.1 0.2 eq.29
  8.2 0.2 eq.25
  8.4 4.5 %reduce-window.6 = s32[16,8,128]{2,1,0:T(8,128)S(1)} reduce-window(s32[16,8,128]{2,1,0:T(8,128)S(1)} %fusion.94, s32[]{:T(128)} %constant.17.clone.1), window={size=1x1x128 pad=0_0x0_0x127_0}, to_apply=%region_0.0 | reduce-window | flops 2080768 | bytes 131076 | tf_op jit(solution)/shard_map/reduce-window
  13.0 0.1 copy.50
  13.4 0.2 sub.24
  13.6 0.2 mul.133
  13.8 4.3 %scatter_custom_fusion = s32[2048]{0:T(1024)S(1)} fusion(s32[1024]{0:T(1024)S(1)} %bitcast.156, s32[1024]{0:T(1024)S(1)} %add_select_fusion, s32[]{:T(128)} %constant.15.clone.1), kind=kCustom, calls=%fused_computation.131 | custom fusion | bytes 8196 | tf_op jit(solution)/shard_map/scatter | solution.py:73
  18.3 0.1 copy.63
  18.5 6.2 %gather_fusion.1 = bf16[2048,96]{1,0:T(8,128)(2,1)S(1)} fusion(bf16[96,513]{0,1:T(8,128)(2,1)S(1)} %concatenate.25.clone, s32[2048]{0:T(1024)S(1)} %fusion.95), kind=kCustom, calls=%fused_computation.1 | custom fusion | bytes 794624 | tf_op jit(solution)/shard_map/gather | solution.py:79
  24.7 0.3 copy.56
  24.9 13.0 %all_gather.13 = bf16[96,16,256]{2,0,1:T(8,128)(2,1)} all-gather(bf16[96,16,128]{2,0,1:T(8,128)(2,1)S(1)} %copy.56), channel_id=1, replica_groups=mesh['ctx'=2,'exp'=16] {'ctx'}, dimensions={2}, use_global_device_ids=true | all-gather | bytes 1179648 | tf_op jit(solution)/shard_map/all_gather | solution.py:89
  37.9 6.2 %all-to-all-start.1 = ((bf16[96,16,256]{2,0,1:T(8,128)(2,1)}), bf16[96,16,256]{2,0,1:T(8,128)(2,1)S(1)}, u32[]{:S(2)}, u32[]{:S(2)}) async-start(bf16[96,16,256]{2,0,1:T(8,128)(2,1)} %all_gather.13), calls=%async_computation.1 | async-start | bytes 1572864 | tf_op jit(solution)/shard_map/all_to_all | solution.py:93
  44.2 5.5 %gather_fusion = f32[2048,96]{1,0:T(8,128)S(1)} fusion(f32[96,513]{0,1:T(8,128)S(1)} %concatenate.24.clone, s32[2048]{0:T(1024)S(1)} %fusion.95), kind=kCustom, calls=%fused_computation | custom fusion | bytes 1581056 | tf_op jit(solution)/shard_map/gather | solution.py:81
  49.7 0.3 copy.54
  50.0 0.3 copy-done.12
  50.4 0.1 copy.53
  50.5 0.2 reshape.134
  50.7 4.3 %scatter_custom_fusion.1 = f32[2048]{0:T(1024)S(1)} fusion(s32[1024]{0:T(1024)S(1)} %bitcast.157, f32[1024]{0:T(1024)S(1)} %reshape.134, f32[]{:T(128)} %constant.14.clone.1), kind=kCustom, calls=%fused_computation.129 | custom fusion | bytes 8196 | tf_op jit(solution)/shard_map/scatter | solution.py:75
  55.1 12.2 %all_gather.12 = bf16[96,16,256]{2,0,1:T(8,128)(2,1)} all-gather(bf16[96,16,128]{2,0,1:T(8,128)(2,1)S(1)} %multiply_convert_fusion.2), channel_id=1, replica_groups=mesh['ctx'=2,'exp'=16] {'ctx'}, dimensions={2}, use_global_device_ids=true | all-gather | bytes 1179648 | tf_op jit(solution)/shard_map/all_gather | solution.py:90
  67.3 5.7 %all-to-all-start = ((bf16[96,16,256]{2,0,1:T(8,128)(2,1)}), bf16[96,16,256]{2,0,1:T(8,128)(2,1)S(1)}, u32[]{:S(2)}, u32[]{:S(2)}) async-start(bf16[96,16,256]{2,0,1:T(8,128)(2,1)} %all_gather.12), calls=%async_computation | async-start | bytes 1572864 | tf_op jit(solution)/shard_map/all_to_all | solution.py:94
  73.1 4.9 %fusion.14 = f32[1536,256]{0,1:T(8,128)} fusion(bf16[1536,256]{1,0:T(8,128)(2,1)S(1)} %bitcast.148, bf16[1,1536,1536]{2,1,0:T(8,128)(2,1)} %param.14), kind=kOutput, calls=%fused_computation.18 | convolution fusion | flops 1207959552 | bytes 7077888 | tf_op jit(solution)/shard_map/dot_general | solution.py:38
  78.0 13.8 %all-to-all-done = bf16[96,16,256]{2,0,1:T(8,128)(2,1)S(1)} async-done(((bf16[96,16,256]{2,0,1:T(8,128)(2,1)}), bf16[96,16,256]{2,0,1:T(8,128)(2,1)S(1)}, u32[]{:S(2)}, u32[]{:S(2)}) %all-to-all-start) | async-done | bytes 786464 | tf_op jit(solution)/shard_map/all_to_all | solution.py:94
  91.8 5.1 %fusion.20 = bf16[1536,256]{0,1:T(8,128)(2,1)S(1)} fusion(bf16[1536,256]{1,0:T(8,128)(2,1)S(1)} %bitcast.150, bf16[1,1536,1536]{2,1,0:T(8,128)(2,1)} %param.15, f32[1536,256]{0,1:T(8,128)} %fusion.14), kind=kOutput, calls=%fused_computation.20 | convolution fusion | flops 1215430656 | bytes 7864320 | tf_op jit(solution)/shard_map/dot_general | solution.py:50
  96.9 0.9 copy-done.13
  97.8 4.9 %fusion.17 = f32[1536,1,256]{0,2,1:T(8,128)} fusion(bf16[1536,256]{0,1:T(8,128)(2,1)S(1)} %fusion.20, bf16[1,1536,1536]{2,1,0:T(8,128)(2,1)} %param.14), kind=kOutput, calls=%fused_computation.19 | convolution fusion | flops 1207959552 | bytes 7077888 | tf_op jit(solution)/shard_map/dot_general | solution.py:53
  102.7 3.6 %copy.57 = f32[1536,1,256]{2,1,0:T(1,128)S(1)} copy(f32[1536,1,256]{0,2,1:T(8,128)} %fusion.17) | data formatting | bytes 3145728 | tf_op jit(solution)/shard_map/reshape | solution.py:102
  106.3 41.4 %all_to_all.48 = f32[1536,1,256]{2,1,0:T(1,128)S(1)} all-to-all(f32[1536,1,256]{2,1,0:T(1,128)S(1)} %copy.57), channel_id=1, replica_groups=mesh['ctx'=2,'exp'=16] {'exp'}, dimensions={0} | all-to-all | bytes 3145728 | tf_op jit(solution)/shard_map/all_to_all | solution.py:101
  147.6 1.2 copy.61
  149.0 0.3 fusion.73
  149.3 26.2 %reduce-scatter.3.cloned.1.call-done = f32[96,16,128]{2,0,1:T(8,128)} async-done(((f32[96,16,256]{2,0,1:T(8,128)}), f32[96,16,128]{2,0,1:T(8,128)}) %reduce-scatter.3.cloned.1.call-update) | async-done | bytes 786448 | tf_op jit(solution)/shard_map/reduce_scatter | solution.py:108
  175.5 1.2 convert_convert_fusion
  176.7 0.3 copy.58
  177.0 1.0 gather_fusion.2
  178.1 0.1 copy.59
  178.2 1.0 gather_fusion.3
  179.3 0.1 copy.60
  179.4 0.8 fusion.83
  180.4 2.2 collective-permute-start.2
  182.6 1.3 collective-permute-start.3
  183.9 0.2 reduce-scatter.5.cloned.1.call-start
  184.2 4.1 %collective-permute-done.3 = bf16[96,2]{1,0:T(8,128)(2,1)S(1)} collective-permute-done((bf16[96,2]{1,0:T(8,128)(2,1)S(1)}, bf16[96,2]{1,0:T(8,128)(2,1)S(1)}, u32[]{:S(2)}, u32[]{:S(2)}) %collective-permute-start.3) | collective-permute-done | bytes 416 | tf_op jit(solution)/shard_map/ppermute | solution.py:17
  188.3 31.7 %all-gather.3.cloned.1.call-done = bf16[1536,512]{1,0:T(8,128)(2,1)} async-done(((bf16[96,512]{1,0:T(8,128)(2,1)}), bf16[1536,512]{1,0:T(8,128)(2,1)}) %all-gather.3.cloned.1.call-update) | async-done | bytes 1572880 | tf_op jit(solution)/shard_map/all_gather | solution.py:119
  220.1 2.9 fusion.24
  222.9 1.3 fusion.26
  224.3 1.3 fusion.28
  225.6 1.3 fusion.30
  226.9 1.3 fusion.32
  228.3 4.9 %fusion = bf16[1,1536,1536]{2,1,0:T(8,128)(2,1)} fusion(bf16[1536,256]{1,0:T(8,128)(2,1)S(1)} %bitcast.149, bf16[1536,256]{0,1:T(8,128)(2,1)} %copy-done.13), kind=kOutput, calls=%fused_computation.8 | convolution fusion | flops 1210318848 | bytes 6291456 | tf_op jit(solution)/shard_map/dot_general | solution.py:38
  233.2 3.9 %fusion.1 = bf16[1,1536,1536]{2,1,0:T(8,128)(2,1)} fusion(bf16[1536,256]{1,0:T(8,128)(2,1)S(1)} %bitcast.151, f32[1536,256]{0,1:T(8,128)S(1)} %copy-done.14), kind=kOutput, calls=%fused_computation.9 | convolution fusion | flops 1213857792 | bytes 7077888 | tf_op jit(solution)/shard_map/dot_general | solution.py:38
  237.1 1.1 fusion.112
  238.2 1.3 collective-permute-start
  239.5 6.0 %collective-permute-start.1 = (bf16[1536,2]{1,0:T(8,128)(2,1)}, bf16[1536,2]{1,0:T(8,128)(2,1)}, u32[]{:S(2)}, u32[]{:S(2)}) collective-permute-start(bf16[1536,2]{1,0:T(8,128)(2,1)} %get-tuple-element.7), channel_id=1, source_target_pairs={{0,16},{1,17},{2,18},{3,19},{4,20},{5,21},{6,22},{7,23},{8,24},{9,... | collective-permute-start | bytes 18440 | tf_op jit(solution)/shard_map/ppermute | solution.py:15
  245.6 4.5 %all-gather.5.cloned.1.call-done = bf16[5,96,1536]{2,1,0:T(8,128)(2,1)} async-done(((bf16[5,96,768]{2,1,0:T(8,128)(2,1)}), bf16[5,96,1536]{2,1,0:T(8,128)(2,1)}) %all-gather.5.cloned.1.call-update) | async-done | bytes 1474576 | tf_op jit(solution)/shard_map/all_gather | solution.py:117
  250.1 1.5 fusion.72
  251.6 2.0 collective-permute-done.1
  253.6 1.7 fusion.39
  255.3 1.1 constant_dynamic-update-slice_fusion
  256.4 0.6 fusion.41
  257.1 0.6 fusion.62
  257.7 0.2 copy-done.5
  258.1 2.4 fusion.65
  260.5 19.5 %reduce-scatter.5.cloned.1.call-done = bf16[5,96,768]{2,1,0:T(8,128)(2,1)} async-done(((bf16[5,96,1536]{2,1,0:T(8,128)(2,1)}), bf16[5,96,768]{2,1,0:T(8,128)(2,1)}) %reduce-scatter.5.cloned.1.call-update) | async-done | bytes 737296 | tf_op jit(solution)/shard_map/reduce_scatter | solution.py:139
  280.0 2.3 convert_element_type.80
  (59 shorter events, 1.3 us)
Async XLA Ops:
  7.2 11.0 %copy-start.1 = (bf16[96,512]{1,0:T(8,128)(2,1)S(1)}, bf16[96,512]{1,0:T(8,128)(2,1)}, u32[]{:S(2)}) copy-start(bf16[96,512]{1,0:T(8,128)(2,1)} %param.8) | copy-start | bytes 294916
  7.2 11.0 %copy-start.8 = (bf16[96,512]{1,0:T(8,128)(2,1)S(1)}, bf16[96,512]{1,0:T(8,128)(2,1)}, u32[]{:S(2)}) copy-start(bf16[96,512]{1,0:T(8,128)(2,1)} %param.9) | copy-start | bytes 294916
  24.9 19.2 %copy-start.9 = (bf16[96,512]{1,0:T(8,128)(2,1)S(1)}, bf16[96,512]{1,0:T(8,128)(2,1)}, u32[]{:S(2)}) copy-start(bf16[96,512]{1,0:T(8,128)(2,1)} %param.10) | copy-start | bytes 294916
  37.9 29.5 %all-to-all-start.1 = ((bf16[96,16,256]{2,0,1:T(8,128)(2,1)}), bf16[96,16,256]{2,0,1:T(8,128)(2,1)S(1)}, u32[]{:S(2)}, u32[]{:S(2)}) async-start(bf16[96,16,256]{2,0,1:T(8,128)(2,1)} %all_gather.13), calls=%async_computation.1 | async-start | bytes 1572864 | tf_op jit(solution)/shard_map/all_to_all | solution.py:93
  49.7 0.7 copy-start.12
  67.3 24.4 %all-to-all-start = ((bf16[96,16,256]{2,0,1:T(8,128)(2,1)}), bf16[96,16,256]{2,0,1:T(8,128)(2,1)S(1)}, u32[]{:S(2)}, u32[]{:S(2)}) async-start(bf16[96,16,256]{2,0,1:T(8,128)(2,1)} %all_gather.12), calls=%async_computation | async-start | bytes 1572864 | tf_op jit(solution)/shard_map/all_to_all | solution.py:94
  73.1 102.4 %reduce-scatter.3.cloned.1.call-start = ((), (), s32[]{:S(2)}) async-start(), calls=%async_computation.5 | async-start | bytes 2359296 | tf_op jit(solution)/shard_map/reduce_scatter | solution.py:108
  91.8 5.1 %copy-start.2 = (bf16[96,16,256]{2,0,1:T(8,128)(2,1)}, bf16[96,16,256]{2,0,1:T(8,128)(2,1)S(1)}, u32[]{:S(2)}) copy-start(bf16[96,16,256]{2,0,1:T(8,128)(2,1)S(1)} %all-to-all-done) | copy-start | bytes 2359300
  96.9 0.9 copy-start.13
  148.9 71.2 %all-gather.3.cloned.1.call-start = ((), (), s32[]{:S(2)}) async-start(), calls=%async_computation.6 | async-start | bytes 1671168 | tf_op jit(solution)/shard_map/all_gather | solution.py:119
  178.2 5.7 %copy-start.4 = (f32[512,96]{0,1:T(8,128)}, f32[512,96]{0,1:T(8,128)S(1)}, u32[]{:S(2)}) copy-start(f32[512,96]{0,1:T(8,128)S(1)} %copy.59) | copy-start | bytes 589828
  179.4 8.9 %copy-start.6 = (f32[512,96]{0,1:T(8,128)}, f32[512,96]{0,1:T(8,128)S(1)}, u32[]{:S(2)}) copy-start(f32[512,96]{0,1:T(8,128)S(1)} %copy.60) | copy-start | bytes 589828
  180.2 69.9 %all-gather.5.cloned.1.call-start = ((), (), s32[]{:S(2)}) async-start(), calls=%async_computation.7 | async-start | bytes 2211840 | tf_op jit(solution)/shard_map/all_gather | solution.py:117
  180.4 8.0 %collective-permute-start.2 = (bf16[96,2]{1,0:T(8,128)(2,1)S(1)}, bf16[96,2]{1,0:T(8,128)(2,1)S(1)}, u32[]{:S(2)}, u32[]{:S(2)}) collective-permute-start(bf16[96,2]{1,0:T(8,128)(2,1)S(1)} %get-tuple-element.11), channel_id=1, source_target_pairs={{0,16},{1,17},{2,18},{3,19},{4,20},{5,21},{6,22},{7,23},{8,24},{9,... | collective-permute-start | bytes 1160 | tf_op jit(solution)/shard_map/ppermute | solution.py:15
  182.6 5.7 %collective-permute-start.3 = (bf16[96,2]{1,0:T(8,128)(2,1)S(1)}, bf16[96,2]{1,0:T(8,128)(2,1)S(1)}, u32[]{:S(2)}, u32[]{:S(2)}) collective-permute-start(bf16[96,2]{1,0:T(8,128)(2,1)S(1)} %get-tuple-element.10), channel_id=1, source_target_pairs={{16,0},{17,1},{18,2},{19,3},{20,4},{21,5},{22,6},{23,7},{24,8},{25... | collective-permute-start | bytes 1160 | tf_op jit(solution)/shard_map/ppermute | solution.py:17
  183.9 96.1 %reduce-scatter.5.cloned.1.call-start = ((), (), s32[]{:S(2)}) async-start(), calls=%async_computation.8 | async-start | bytes 2211840 | tf_op jit(solution)/shard_map/reduce_scatter | solution.py:139
  220.1 2.9 copy-start
  228.3 5.0 %copy-start.3 = (bf16[96,16,256]{2,0,1:T(8,128)(2,1)S(1)}, bf16[96,16,256]{2,0,1:T(8,128)(2,1)}, u32[]{:S(2)}) copy-start(bf16[96,16,256]{2,0,1:T(8,128)(2,1)} %copy-done.2) | copy-start | bytes 2359300
  228.3 5.0 %copy-start.14 = (f32[1536,256]{0,1:T(8,128)S(1)}, f32[1536,256]{0,1:T(8,128)}, u32[]{:S(2)}) copy-start(f32[1536,256]{0,1:T(8,128)} %fusion.14) | copy-start | bytes 4718596
  238.2 17.1 %collective-permute-start = (bf16[1536,2]{1,0:T(8,128)(2,1)}, bf16[1536,2]{1,0:T(8,128)(2,1)}, u32[]{:S(2)}, u32[]{:S(2)}) collective-permute-start(bf16[1536,2]{1,0:T(8,128)(2,1)} %get-tuple-element.6), channel_id=1, source_target_pairs={{16,0},{17,1},{18,2},{19,3},{20,4},{21,5},{22,6},{23,7},{24,8},{25... | collective-permute-start | bytes 18440 | tf_op jit(solution)/shard_map/ppermute | solution.py:17
  239.5 14.1 %collective-permute-start.1 = (bf16[1536,2]{1,0:T(8,128)(2,1)}, bf16[1536,2]{1,0:T(8,128)(2,1)}, u32[]{:S(2)}, u32[]{:S(2)}) collective-permute-start(bf16[1536,2]{1,0:T(8,128)(2,1)} %get-tuple-element.7), channel_id=1, source_target_pairs={{0,16},{1,17},{2,18},{3,19},{4,20},{5,21},{6,22},{7,23},{8,24},{9,... | collective-permute-start | bytes 18440 | tf_op jit(solution)/shard_map/ppermute | solution.py:15
  250.1 3.5 %copy-start.11 = (bf16[5,96,1536]{2,1,0:T(8,128)(2,1)S(1)}, bf16[5,96,1536]{2,1,0:T(8,128)(2,1)}, u32[]{:S(2)}) copy-start(bf16[5,96,1536]{2,1,0:T(8,128)(2,1)} %all-gather.5.cloned.1.call-done) | copy-start | bytes 4423684
  257.0 0.9 copy-start.5
  257.0 1.0 copy-start.7
  257.0 1.1 copy-start.10
Sparse Core Ops, SparseCore 0:
  149.0 26.4 reduce-scatter.2
  180.4 39.6 all-gather.2
  221.7 28.3 all-gather.4
  252.9 27.0 reduce-scatter.4
where the time goes:
time: 290 us; the launch traced here: 289 us
  waiting for transfers between devices  102 us (35%)
  blocking collectives  66.6 us (23%)
  matrix products  38.7 us (13%)
  local copies, waits for them, and re-layouts  34.8 us (12%)
  starting transfers between devices  23.1 us (8%)
  between operations  14.3 us (5%)
  other arithmetic  9.54 us (3%)
    all_to_all x1, blocking collectives, local(): lax.all_to_all(rows_back.reshape(model_width, 1, total_rows), 'exp', spli...  41.4 us
    all_gather x1, waiting for transfers between devices, local(): gathered = lax.all_gather(grad_pre_conv, 'exp', axis=0, tiled=True)  31.7 us
    reduce_scatter x1, waiting for transfers between devices, local(): lax.psum_scatter(moved_back, 'ctx', scatter_dimension=2, tiled=True)  26.2 us
    dot_general x8, matrix products, turned(): lax.dot_general(left.astype(jnp.float32), right.astype(jnp.float32), (dim...  21.9 us
    reduce_scatter x1, waiting for transfers between devices, local(): lax.psum_scatter(conv_grad.astype(jnp.bfloat16), 'ctx', scatter_dimension...  19.5 us
    all_to_all x1, waiting for transfers between devices, local(): lax.all_to_all(copied[1], 'exp', split_axis=1, concat_axis=0, tiled=True)  13.8 us
    all_gather x1, blocking collectives, local(): lax.all_gather(send_rows, 'ctx', axis=2, tiled=True)  13 us
    all_gather x1, blocking collectives, local(): lax.all_gather(send_grad, 'ctx', axis=2, tiled=True)  12.2 us
  transfers between devices with their start and end apart: 10, of which 7 were waited for; matrix products, arithmetic and copies ran while one was open for 15% of the time, Pallas kernels for 0%

commit v1 on v0

--- a/solution.py
+++ b/solution.py
@@ -116,7 +116,40 @@
     grad_pre_conv = (grad_total * gelu_slope(pre_float)).astype(jnp.bfloat16)
     full_weight = lax.all_gather(conv_weight, "ctx", axis=2, tiled=True)
     rim_inputs = with_halo(inputs, (("ctx", 1),), margin)
-    gathered = lax.all_gather(grad_pre_conv, "exp", axis=0, tiled=True)
+    local_part, local_out, work_now = (
+        jax.lax.axis_size("exp"),
+        jax.lax.axis_index("exp"),
+        grad_pre_conv.shape[0],
+    )
+    gathered = lax.dynamic_update_slice_in_dim(
+        jnp.zeros(
+            [
+                dev_i * local_part if j == 0 else dev_i
+                for j, dev_i in enumerate(grad_pre_conv.shape)
+            ],
+            grad_pre_conv.dtype,
+        ),
+        grad_pre_conv,
+        local_out * work_now,
+        axis=0,
+    )
+    t = 1
+    a_next = finding = grad_pre_conv
+    while t < local_part // 2 + 1:
+        a_next = jax.lax.ppermute(
+            a_next, "exp", [(j, (j + 1) % local_part) for j in range(local_part)]
+        )
+        gathered = lax.dynamic_update_slice_in_dim(
+            gathered, a_next, (local_out - t) % local_part * work_now, axis=0
+        )
+        if 2 * t < local_part:
+            finding = jax.lax.ppermute(
+                finding, "exp", [(j, (j - 1) % local_part) for j in range(local_part)]
+            )
+            gathered = lax.dynamic_update_slice_in_dim(
+                gathered, finding, (local_out + t) % local_part * work_now, axis=0
+            )
+        t = t + 1
     rim_grad = with_halo(gathered, (("ctx", 1),), margin)
     conv_back = jnp.zeros((channels, bins_local), jnp.float32)
     tap_grads = []

time: 290 us -> 279 us (0.962)
  waiting for transfers between devices: 102 us -> 69.4 us
  starting transfers between devices: 23.1 us -> 53.7 us
  matrix products: 38.7 us -> 31.3 us
    all_gather x1 -> x0, waiting for transfers between devices: 31.7 us -> none  [local(): gathered = lax.all_gather(grad_pre_conv, 'exp', axis=0, tiled=True)]
    ppermute x0 -> x15, starting transfers between devices: none -> 31.6 us  [the longest x7 31.6 us: local(): jax.lax.ppermute(finding, 'exp', [(j, (j - 1) % local_part) for j in rang...]
    ppermute x0 -> x15, waiting for transfers between devices: none -> 22.3 us  [the longest x8 21.9 us: local(): jax.lax.ppermute(a_next, 'exp', [(j, (j + 1) % local_part) for j in range...]
    reduce_scatter x1, waiting for transfers between devices: 19.5 us -> 0.01 us  [local(): lax.psum_scatter(conv_grad.astype(jnp.bfloat16), 'ctx', scatter_dimension...]
    ppermute x2, waiting for transfers between devices: 2.01 us -> 10.7 us  [with_halo(): lax.ppermute(tail, axis, [(i, (i + 1) % count) for i in range(ends)])]
    reduce_scatter x1, waiting for transfers between devices: 26.2 us -> 19 us  [local(): lax.psum_scatter(moved_back, 'ctx', scatter_dimension=2, tiled=True)]
    dot_general x8, matrix products: 21.9 us -> 15.8 us  [turned(): lax.dot_general(left.astype(jnp.float32), right.astype(jnp.float32), (dim...]
    all_gather x1, waiting for transfers between devices: 4.49 us -> 0.02 us  [local(): full_weight = lax.all_gather(conv_weight, 'ctx', axis=2, tiled=True)]
  transfers between devices with their start and end apart: 10 -> 24, of which waited for: 7 -> 14; matrix products, arithmetic and copies ran while one was open for 15% -> 14% of each run, Pallas kernels for 0% -> 0%
where the time goes in v1:
time: 279 us; the launch traced here: 278 us
  waiting for transfers between devices  69.4 us (25%)
  blocking collectives  66.6 us (24%)
  starting transfers between devices  53.7 us (19%)
  local copies, waits for them, and re-layouts  32.3 us (12%)
  matrix products  31.3 us (11%)
  between operations  14.8 us (5%)
  other arithmetic  9.83 us (4%)
    all_to_all x1, blocking collectives, local(): lax.all_to_all(rows_back.reshape(model_width, 1, total_rows), 'exp', spli...  41.4 us
    ppermute x7, starting transfers between devices, local(): jax.lax.ppermute(finding, 'exp', [(j, (j - 1) % local_part) for j in rang...  31.6 us
    ppermute x8, waiting for transfers between devices, local(): jax.lax.ppermute(a_next, 'exp', [(j, (j + 1) % local_part) for j in range...  21.9 us
    reduce_scatter x1, waiting for transfers between devices, local(): lax.psum_scatter(moved_back, 'ctx', scatter_dimension=2, tiled=True)  19 us
    dot_general x8, matrix products, turned(): lax.dot_general(left.astype(jnp.float32), right.astype(jnp.float32), (dim...  15.8 us
    all_to_all x1, waiting for transfers between devices, local(): lax.all_to_all(copied[1], 'exp', split_axis=1, concat_axis=0, tiled=True)  14.9 us
    all_gather x1, blocking collectives, local(): lax.all_gather(send_rows, 'ctx', axis=2, tiled=True)  13 us
    all_gather x1, blocking collectives, local(): lax.all_gather(send_grad, 'ctx', axis=2, tiled=True)  12.2 us
  transfers between devices with their start and end apart: 24, of which 14 were waited for; matrix products, arithmetic and copies ran while one was open for 14% of the time, Pallas kernels for 0%

profile of v1, /device:TPU:0, one launch (start us, length us, event | category | flops | bytes accessed | tf_op | source)
XLA Modules:
  0.0 277.9 jit_solution(1638088889270176189)
XLA Ops:
  7.2 0.8 copy.47
  8.3 1.0 fusion.65
  9.5 4.5 %reduce-window.6 = s32[16,8,128]{2,1,0:T(8,128)S(1)} reduce-window(s32[16,8,128]{2,1,0:T(8,128)S(1)} %fusion.81, s32[]{:T(128)} %constant.131.clone.1), window={size=1x1x128 pad=0_0x0_0x127_0}, to_apply=%region_0.0 | reduce-window | flops 2080768 | bytes 131076 | tf_op jit(solution)/shard_map/reduce-window
  14.9 4.3 %scatter_custom_fusion = s32[2048]{0:T(1024)S(1)} fusion(s32[1024]{0:T(1024)S(1)} %bitcast.160, s32[1024]{0:T(1024)S(1)} %add_select_fusion, s32[]{:T(128)} %constant.129.clone.1), kind=kCustom, calls=%fused_computation.147 | custom fusion | bytes 8196 | tf_op jit(solution)/shard_map/scatter | solution.py:73
  19.3 6.2 %gather_fusion.1 = bf16[2048,96]{1,0:T(8,128)(2,1)S(1)} fusion(bf16[96,513]{0,1:T(8,128)(2,1)S(1)} %concatenate.25.clone, s32[2048]{0:T(1024)S(1)} %fusion.82), kind=kCustom, calls=%fused_computation.1 | custom fusion | bytes 794624 | tf_op jit(solution)/shard_map/gather | solution.py:79
  25.5 0.2 copy.56
  25.8 13.0 %all_gather.10 = bf16[96,16,256]{2,0,1:T(8,128)(2,1)} all-gather(bf16[96,16,128]{2,0,1:T(8,128)(2,1)S(1)} %copy.56), channel_id=1, replica_groups=mesh['ctx'=2,'exp'=16] {'ctx'}, dimensions={2}, use_global_device_ids=true | all-gather | bytes 1179648 | tf_op jit(solution)/shard_map/all_gather | solution.py:89
  38.7 6.2 %all-to-all-start.1 = ((bf16[96,16,256]{2,0,1:T(8,128)(2,1)}), bf16[96,16,256]{2,0,1:T(8,128)(2,1)S(1)}, u32[]{:S(2)}, u32[]{:S(2)}) async-start(bf16[96,16,256]{2,0,1:T(8,128)(2,1)} %all_gather.10), calls=%async_computation.1 | async-start | bytes 1572864 | tf_op jit(solution)/shard_map/all_to_all | solution.py:93
  45.4 4.3 %scatter_custom_fusion.1 = f32[2048]{0:T(1024)S(1)} fusion(s32[1024]{0:T(1024)S(1)} %bitcast.161, f32[1024]{0:T(1024)S(1)} %reshape.134, f32[]{:T(128)} %constant.128.clone.1), kind=kCustom, calls=%fused_computation.129 | custom fusion | bytes 8196 | tf_op jit(solution)/shard_map/scatter | solution.py:75
  49.7 5.5 %gather_fusion = f32[2048,96]{1,0:T(8,128)S(1)} fusion(f32[96,513]{0,1:T(8,128)S(1)} %concatenate.24.clone, s32[2048]{0:T(1024)S(1)} %fusion.82), kind=kCustom, calls=%fused_computation | custom fusion | bytes 1581056 | tf_op jit(solution)/shard_map/gather | solution.py:81
  55.2 0.3 copy.54
  55.6 12.2 %all_gather.9 = bf16[96,16,256]{2,0,1:T(8,128)(2,1)} all-gather(bf16[96,16,128]{2,0,1:T(8,128)(2,1)S(1)} %multiply_convert_fusion.2), channel_id=1, replica_groups=mesh['ctx'=2,'exp'=16] {'ctx'}, dimensions={2}, use_global_device_ids=true | all-gather | bytes 1179648 | tf_op jit(solution)/shard_map/all_gather | solution.py:90
  67.9 5.7 %all-to-all-start = ((bf16[96,16,256]{2,0,1:T(8,128)(2,1)}), bf16[96,16,256]{2,0,1:T(8,128)(2,1)S(1)}, u32[]{:S(2)}, u32[]{:S(2)}) async-start(bf16[96,16,256]{2,0,1:T(8,128)(2,1)} %all_gather.9), calls=%async_computation | async-start | bytes 1572864 | tf_op jit(solution)/shard_map/all_to_all | solution.py:94
  73.6 3.7 %fusion.14 = f32[1536,256]{0,1:T(8,128)S(1)} fusion(bf16[1536,256]{1,0:T(8,128)(2,1)S(1)} %bitcast.152, bf16[1,1536,1536]{2,1,0:T(8,128)(2,1)} %param.14), kind=kOutput, calls=%fused_computation.18 | convolution fusion | flops 1207959552 | bytes 7077888 | tf_op jit(solution)/shard_map/dot_general | solution.py:38
  77.4 14.9 %all-to-all-done = bf16[96,16,256]{2,0,1:T(8,128)(2,1)S(1)} async-done(((bf16[96,16,256]{2,0,1:T(8,128)(2,1)}), bf16[96,16,256]{2,0,1:T(8,128)(2,1)S(1)}, u32[]{:S(2)}, u32[]{:S(2)}) %all-to-all-start) | async-done | bytes 786464 | tf_op jit(solution)/shard_map/all_to_all | solution.py:94
  92.3 4.6 %fusion.20 = bf16[1536,256]{0,1:T(8,128)(2,1)S(1)} fusion(bf16[1536,256]{1,0:T(8,128)(2,1)S(1)} %bitcast.154, bf16[1,1536,1536]{2,1,0:T(8,128)(2,1)} %param.15, f32[1536,256]{0,1:T(8,128)S(1)} %fusion.14), kind=kOutput, calls=%fused_computation.20 | convolution fusion | flops 1215430656 | bytes 7864320 | tf_op jit(solution)/shard_map/dot_general | solution.py:50
  97.0 0.9 copy-done.14
  97.9 3.8 %fusion.17 = f32[1536,1,256]{0,2,1:T(8,128)S(1)} fusion(bf16[1536,256]{0,1:T(8,128)(2,1)S(1)} %fusion.20, bf16[1,1536,1536]{2,1,0:T(8,128)(2,1)} %param.14), kind=kOutput, calls=%fused_computation.19 | convolution fusion | flops 1207959552 | bytes 7077888 | tf_op jit(solution)/shard_map/dot_general | solution.py:53
  101.6 1.1 copy.57
  102.8 41.4 %all_to_all.48 = f32[1536,1,256]{2,1,0:T(1,128)S(1)} all-to-all(f32[1536,1,256]{2,1,0:T(1,128)S(1)} %copy.57), channel_id=1, replica_groups=mesh['ctx'=2,'exp'=16] {'exp'}, dimensions={0} | all-to-all | bytes 3145728 | tf_op jit(solution)/shard_map/all_to_all | solution.py:101
  144.1 1.2 copy.61
  145.4 0.8 copy-done
  146.3 1.3 collective-permute-start.18
  147.6 4.5 %collective-permute-start.17 = (bf16[96,2]{1,0:T(8,128)(2,1)S(1)}, bf16[96,2]{1,0:T(8,128)(2,1)S(1)}, u32[]{:S(2)}, u32[]{:S(2)}) collective-permute-start(bf16[96,2]{1,0:T(8,128)(2,1)S(1)} %get-tuple-element.13), channel_id=1, source_target_pairs={{0,16},{1,17},{2,18},{3,19},{4,20},{5,21},{6,22},{7,23},{8,24},{9,... | collective-permute-start | bytes 1160 | tf_op jit(solution)/shard_map/ppermute | solution.py:15
  152.6 0.3 fusion.60
  153.0 19.0 %reduce-scatter.3.cloned.1.call-done = f32[96,16,128]{2,0,1:T(8,128)} async-done(((f32[96,16,256]{2,0,1:T(8,128)}), f32[96,16,128]{2,0,1:T(8,128)}) %reduce-scatter.3.cloned.1.call-update) | async-done | bytes 786448 | tf_op jit(solution)/shard_map/reduce_scatter | solution.py:108
  172.0 1.2 convert_convert_fusion
  173.2 0.3 copy.58
  173.5 1.0 gather_fusion.3
  174.6 1.0 gather_fusion.2
  176.0 0.5 copy-done.5
  176.8 4.4 %collective-permute-start.1 = (bf16[96,512]{1,0:T(8,128)(2,1)S(1)}, bf16[96,512]{1,0:T(8,128)(2,1)S(1)}, u32[]{:S(2)}, u32[]{:S(2)}) collective-permute-start(bf16[96,512]{1,0:T(8,128)(2,1)S(1)} %get-tuple-element.7), channel_id=1, source_target_pairs={{0,15},{1,0},{2,1},{3,2},{4,3},{5,4},{6,5},{7,6},{8,7},{9,8},{10,9... | collective-permute-start | bytes 294920 | tf_op jit(solution)/shard_map/ppermute | solution.py:146
  181.3 2.4 collective-permute-done
  183.6 4.4 %collective-permute-start.3 = (bf16[96,512]{1,0:T(8,128)(2,1)S(1)}, bf16[96,512]{1,0:T(8,128)(2,1)S(1)}, u32[]{:S(2)}, u32[]{:S(2)}) collective-permute-start(bf16[96,512]{1,0:T(8,128)(2,1)S(1)} %collective-permute-done.1), channel_id=1, source_target_pairs={{0,15},{1,0},{2,1},{3,2},{4,3},{5,4},{6,5},{7,6},{8,7},{9,8},{10,9... | collective-permute-start | bytes 294920 | tf_op jit(solution)/shard_map/ppermute | solution.py:146
  188.1 2.3 collective-permute-done.2
  190.4 4.4 %collective-permute-start.5 = (bf16[96,512]{1,0:T(8,128)(2,1)S(1)}, bf16[96,512]{1,0:T(8,128)(2,1)S(1)}, u32[]{:S(2)}, u32[]{:S(2)}) collective-permute-start(bf16[96,512]{1,0:T(8,128)(2,1)S(1)} %collective-permute-done.3), channel_id=1, source_target_pairs={{0,15},{1,0},{2,1},{3,2},{4,3},{5,4},{6,5},{7,6},{8,7},{9,8},{10,9... | collective-permute-start | bytes 294920 | tf_op jit(solution)/shard_map/ppermute | solution.py:146
  194.9 2.4 collective-permute-done.4
  197.2 4.4 %collective-permute-start.7 = (bf16[96,512]{1,0:T(8,128)(2,1)S(1)}, bf16[96,512]{1,0:T(8,128)(2,1)S(1)}, u32[]{:S(2)}, u32[]{:S(2)}) collective-permute-start(bf16[96,512]{1,0:T(8,128)(2,1)S(1)} %collective-permute-done.5), channel_id=1, source_target_pairs={{0,15},{1,0},{2,1},{3,2},{4,3},{5,4},{6,5},{7,6},{8,7},{9,8},{10,9... | collective-permute-start | bytes 294920 | tf_op jit(solution)/shard_map/ppermute | solution.py:146
  201.7 2.3 collective-permute-done.6
  204.0 4.5 %collective-permute-start.9 = (bf16[96,512]{1,0:T(8,128)(2,1)S(1)}, bf16[96,512]{1,0:T(8,128)(2,1)S(1)}, u32[]{:S(2)}, u32[]{:S(2)}) collective-permute-start(bf16[96,512]{1,0:T(8,128)(2,1)S(1)} %collective-permute-done.7), channel_id=1, source_target_pairs={{0,15},{1,0},{2,1},{3,2},{4,3},{5,4},{6,5},{7,6},{8,7},{9,8},{10,9... | collective-permute-start | bytes 294920 | tf_op jit(solution)/shard_map/ppermute | solution.py:146
  208.5 2.1 collective-permute-done.8
  210.7 4.6 %collective-permute-start.11 = (bf16[96,512]{1,0:T(8,128)(2,1)S(1)}, bf16[96,512]{1,0:T(8,128)(2,1)S(1)}, u32[]{:S(2)}, u32[]{:S(2)}) collective-permute-start(bf16[96,512]{1,0:T(8,128)(2,1)S(1)} %collective-permute-done.9), channel_id=1, source_target_pairs={{0,15},{1,0},{2,1},{3,2},{4,3},{5,4},{6,5},{7,6},{8,7},{9,8},{10,9... | collective-permute-start | bytes 294920 | tf_op jit(solution)/shard_map/ppermute | solution.py:146
  215.4 2.1 collective-permute-done.10
  217.6 4.6 %collective-permute-start.13 = (bf16[96,512]{1,0:T(8,128)(2,1)S(1)}, bf16[96,512]{1,0:T(8,128)(2,1)S(1)}, u32[]{:S(2)}, u32[]{:S(2)}) collective-permute-start(bf16[96,512]{1,0:T(8,128)(2,1)S(1)} %collective-permute-done.11), channel_id=1, source_target_pairs={{0,15},{1,0},{2,1},{3,2},{4,3},{5,4},{6,5},{7,6},{8,7},{9,8},{10,9... | collective-permute-start | bytes 294920 | tf_op jit(solution)/shard_map/ppermute | solution.py:146
  222.2 2.0 collective-permute-done.12
  224.4 6.5 %collective-permute-done.14 = bf16[96,512]{1,0:T(8,128)(2,1)S(1)} collective-permute-done((bf16[96,512]{1,0:T(8,128)(2,1)S(1)}, bf16[96,512]{1,0:T(8,128)(2,1)S(1)}, u32[]{:S(2)}, u32[]{:S(2)}) %collective-permute-start.14) | collective-permute-done | bytes 98336 | tf_op jit(solution)/shard_map/ppermute | solution.py:139
  231.0 0.6 fusion.24
  231.6 0.6 fusion.26
  232.2 0.6 fusion.28
  232.9 0.6 fusion.30
  233.5 0.6 fusion.32
  234.1 1.1 copy-done.1
  235.2 5.5 %fusion.1 = bf16[1,1536,1536]{2,1,0:T(8,128)(2,1)} fusion(bf16[1536,256]{1,0:T(8,128)(2,1)} %bitcast.155, f32[1536,256]{0,1:T(8,128)} %copy-done.16), kind=kOutput, calls=%fused_computation.9 | convolution fusion | flops 1213857792 | bytes 7077888 | tf_op jit(solution)/shard_map/dot_general | solution.py:38
  240.9 2.9 %collective-permute-start.16 = (bf16[1536,2]{1,0:T(8,128)(2,1)S(1)}, bf16[1536,2]{1,0:T(8,128)(2,1)S(1)}, u32[]{:S(2)}, u32[]{:S(2)}) collective-permute-start(bf16[1536,2]{1,0:T(8,128)(2,1)S(1)} %get-tuple-element.9), channel_id=1, source_target_pairs={{0,16},{1,17},{2,18},{3,19},{4,20},{5,21},{6,22},{7,23},{8,24},{9,... | collective-permute-start | bytes 18440 | tf_op jit(solution)/shard_map/ppermute | solution.py:15
  243.8 3.6 %fusion = bf16[1,1536,1536]{2,1,0:T(8,128)(2,1)} fusion(bf16[1536,256]{1,0:T(8,128)(2,1)S(1)} %bitcast.153, bf16[1536,256]{0,1:T(8,128)(2,1)S(1)} %copy-done.15), kind=kOutput, calls=%fused_computation.8 | convolution fusion | flops 1210318848 | bytes 6291456 | tf_op jit(solution)/shard_map/dot_general | solution.py:38
  247.4 1.3 collective-permute-start.15
  248.7 10.7 %collective-permute-done.16 = bf16[1536,2]{1,0:T(8,128)(2,1)S(1)} collective-permute-done((bf16[1536,2]{1,0:T(8,128)(2,1)S(1)}, bf16[1536,2]{1,0:T(8,128)(2,1)S(1)}, u32[]{:S(2)}, u32[]{:S(2)}) %collective-permute-start.16) | collective-permute-done | bytes 6176 | tf_op jit(solution)/shard_map/ppermute | solution.py:15
  259.4 1.7 fusion.40
  261.1 0.8 fusion.46
  261.9 2.4 collective-permute-done.15
  264.3 1.8 fusion.42
  266.1 1.8 fusion.48
  267.9 1.0 fusion.55
  269.0 2.3 convert_element_type.80
  (104 shorter events, 3.6 us)
Async XLA Ops:
  25.8 19.2 %copy-start.13 = (f32[512,2]{0,1:T(2,128)S(1)}, f32[512,2]{0,1:T(2,128)}, u32[]{:S(2)}) copy-start(f32[512,2]{0,1:T(2,128)} %param.13) | copy-start | bytes 12292
  25.8 19.5 %copy-start.4 = (bf16[96,512]{1,0:T(8,128)(2,1)S(1)}, bf16[96,512]{1,0:T(8,128)(2,1)}, u32[]{:S(2)}) copy-start(bf16[96,512]{1,0:T(8,128)(2,1)} %param.10) | copy-start | bytes 294916
  38.7 29.1 %all-to-all-start.1 = ((bf16[96,16,256]{2,0,1:T(8,128)(2,1)}), bf16[96,16,256]{2,0,1:T(8,128)(2,1)S(1)}, u32[]{:S(2)}, u32[]{:S(2)}) async-start(bf16[96,16,256]{2,0,1:T(8,128)(2,1)} %all_gather.10), calls=%async_computation.1 | async-start | bytes 1572864 | tf_op jit(solution)/shard_map/all_to_all | solution.py:93
  67.8 9.5 %copy-start.6 = (bf16[96,16,256]{2,0,1:T(8,128)(2,1)}, bf16[96,16,256]{2,0,1:T(8,128)(2,1)S(1)}, u32[]{:S(2)}) copy-start(bf16[96,16,256]{2,0,1:T(8,128)(2,1)S(1)} %all-to-all-done.1) | copy-start | bytes 2359300
  67.9 24.4 %all-to-all-start = ((bf16[96,16,256]{2,0,1:T(8,128)(2,1)}), bf16[96,16,256]{2,0,1:T(8,128)(2,1)S(1)}, u32[]{:S(2)}, u32[]{:S(2)}) async-start(bf16[96,16,256]{2,0,1:T(8,128)(2,1)} %all_gather.9), calls=%async_computation | async-start | bytes 1572864 | tf_op jit(solution)/shard_map/all_to_all | solution.py:94
  73.6 98.4 %reduce-scatter.3.cloned.1.call-start = ((), (), s32[]{:S(2)}) async-start(), calls=%async_computation.5 | async-start | bytes 2359296 | tf_op jit(solution)/shard_map/reduce_scatter | solution.py:108
  77.4 14.9 %copy-start.16 = (f32[1536,256]{0,1:T(8,128)}, f32[1536,256]{0,1:T(8,128)S(1)}, u32[]{:S(2)}) copy-start(f32[1536,256]{0,1:T(8,128)S(1)} %fusion.14) | copy-start | bytes 4718596
  92.3 4.7 %copy-start.8 = (bf16[96,16,256]{2,0,1:T(8,128)(2,1)}, bf16[96,16,256]{2,0,1:T(8,128)(2,1)S(1)}, u32[]{:S(2)}) copy-start(bf16[96,16,256]{2,0,1:T(8,128)(2,1)S(1)} %all-to-all-done) | copy-start | bytes 2359300
  97.0 0.9 copy-start.14
  145.4 0.9 copy-start
  145.4 103.3 %all-gather.2.cloned.1.call-start = ((), (), s32[]{:S(2)}) async-start(), calls=%async_computation.6 | async-start | bytes 2211840 | tf_op jit(solution)/shard_map/all_gather | solution.py:117
  146.3 34.9 %collective-permute-start.18 = (bf16[96,2]{1,0:T(8,128)(2,1)S(1)}, bf16[96,2]{1,0:T(8,128)(2,1)S(1)}, u32[]{:S(2)}, u32[]{:S(2)}) collective-permute-start(bf16[96,2]{1,0:T(8,128)(2,1)S(1)} %get-tuple-element.12), channel_id=1, source_target_pairs={{16,0},{17,1},{18,2},{19,3},{20,4},{21,5},{22,6},{23,7},{24,8},{25... | collective-permute-start | bytes 1160 | tf_op jit(solution)/shard_map/ppermute | solution.py:17
  147.6 83.3 %collective-permute-start.17 = (bf16[96,2]{1,0:T(8,128)(2,1)S(1)}, bf16[96,2]{1,0:T(8,128)(2,1)S(1)}, u32[]{:S(2)}, u32[]{:S(2)}) collective-permute-start(bf16[96,2]{1,0:T(8,128)(2,1)S(1)} %get-tuple-element.13), channel_id=1, source_target_pairs={{0,16},{1,17},{2,18},{3,19},{4,20},{5,21},{6,22},{7,23},{8,24},{9,... | collective-permute-start | bytes 1160 | tf_op jit(solution)/shard_map/ppermute | solution.py:15
  152.2 116.8 %reduce-scatter.5.cloned.1.call-start = ((), (), s32[]{:S(2)}) async-start(), calls=%async_computation.7 | async-start | bytes 2211840 | tf_op jit(solution)/shard_map/reduce_scatter | solution.py:172
  175.6 0.9 copy-start.5
  175.6 0.9 copy-start.11
  175.9 18.9 %copy-start.2 = (f32[512,96]{0,1:T(8,128)}, f32[512,96]{0,1:T(8,128)S(1)}, u32[]{:S(2)}) copy-start(f32[512,96]{0,1:T(8,128)S(1)} %copy.60) | copy-start | bytes 589828
  176.7 6.9 %collective-permute-start = (bf16[96,512]{1,0:T(8,128)(2,1)S(1)}, bf16[96,512]{1,0:T(8,128)(2,1)S(1)}, u32[]{:S(2)}, u32[]{:S(2)}) collective-permute-start(bf16[96,512]{1,0:T(8,128)(2,1)S(1)} %get-tuple-element.7), channel_id=1, source_target_pairs={{0,1},{1,2},{2,3},{3,4},{4,5},{5,6},{6,7},{7,8},{8,9},{9,10},{10,1... | collective-permute-start | bytes 294920 | tf_op jit(solution)/shard_map/ppermute | solution.py:139
  176.8 6.8 %collective-permute-start.1 = (bf16[96,512]{1,0:T(8,128)(2,1)S(1)}, bf16[96,512]{1,0:T(8,128)(2,1)S(1)}, u32[]{:S(2)}, u32[]{:S(2)}) collective-permute-start(bf16[96,512]{1,0:T(8,128)(2,1)S(1)} %get-tuple-element.7), channel_id=1, source_target_pairs={{0,15},{1,0},{2,1},{3,2},{4,3},{5,4},{6,5},{7,6},{8,7},{9,8},{10,9... | collective-permute-start | bytes 294920 | tf_op jit(solution)/shard_map/ppermute | solution.py:146
  181.2 49.7 %copy-start.9 = (bf16[96,514]{1,0:T(8,128)(2,1)}, bf16[96,514]{1,0:T(8,128)(2,1)S(1)}, u32[]{:S(2)}) copy-start(bf16[96,514]{1,0:T(8,128)(2,1)S(1)} %constant_dynamic-update-slice_fusion) | copy-start | bytes 296068
  183.6 6.7 %collective-permute-start.2 = (bf16[96,512]{1,0:T(8,128)(2,1)S(1)}, bf16[96,512]{1,0:T(8,128)(2,1)S(1)}, u32[]{:S(2)}, u32[]{:S(2)}) collective-permute-start(bf16[96,512]{1,0:T(8,128)(2,1)S(1)} %collective-permute-done), channel_id=1, source_target_pairs={{0,1},{1,2},{2,3},{3,4},{4,5},{5,6},{6,7},{7,8},{8,9},{9,10},{10,1... | collective-permute-start | bytes 294920 | tf_op jit(solution)/shard_map/ppermute | solution.py:139
  183.6 6.7 %collective-permute-start.3 = (bf16[96,512]{1,0:T(8,128)(2,1)S(1)}, bf16[96,512]{1,0:T(8,128)(2,1)S(1)}, u32[]{:S(2)}, u32[]{:S(2)}) collective-permute-start(bf16[96,512]{1,0:T(8,128)(2,1)S(1)} %collective-permute-done.1), channel_id=1, source_target_pairs={{0,15},{1,0},{2,1},{3,2},{4,3},{5,4},{6,5},{7,6},{8,7},{9,8},{10,9... | collective-permute-start | bytes 294920 | tf_op jit(solution)/shard_map/ppermute | solution.py:146
  190.4 6.8 %collective-permute-start.4 = (bf16[96,512]{1,0:T(8,128)(2,1)S(1)}, bf16[96,512]{1,0:T(8,128)(2,1)S(1)}, u32[]{:S(2)}, u32[]{:S(2)}) collective-permute-start(bf16[96,512]{1,0:T(8,128)(2,1)S(1)} %collective-permute-done.2), channel_id=1, source_target_pairs={{0,1},{1,2},{2,3},{3,4},{4,5},{5,6},{6,7},{7,8},{8,9},{9,10},{10,1... | collective-permute-start | bytes 294920 | tf_op jit(solution)/shard_map/ppermute | solution.py:139
  190.4 6.8 %collective-permute-start.5 = (bf16[96,512]{1,0:T(8,128)(2,1)S(1)}, bf16[96,512]{1,0:T(8,128)(2,1)S(1)}, u32[]{:S(2)}, u32[]{:S(2)}) collective-permute-start(bf16[96,512]{1,0:T(8,128)(2,1)S(1)} %collective-permute-done.3), channel_id=1, source_target_pairs={{0,15},{1,0},{2,1},{3,2},{4,3},{5,4},{6,5},{7,6},{8,7},{9,8},{10,9... | collective-permute-start | bytes 294920 | tf_op jit(solution)/shard_map/ppermute | solution.py:146
  197.2 6.7 %collective-permute-start.6 = (bf16[96,512]{1,0:T(8,128)(2,1)S(1)}, bf16[96,512]{1,0:T(8,128)(2,1)S(1)}, u32[]{:S(2)}, u32[]{:S(2)}) collective-permute-start(bf16[96,512]{1,0:T(8,128)(2,1)S(1)} %collective-permute-done.4), channel_id=1, source_target_pairs={{0,1},{1,2},{2,3},{3,4},{4,5},{5,6},{6,7},{7,8},{8,9},{9,10},{10,1... | collective-permute-start | bytes 294920 | tf_op jit(solution)/shard_map/ppermute | solution.py:139
  197.2 6.7 %collective-permute-start.7 = (bf16[96,512]{1,0:T(8,128)(2,1)S(1)}, bf16[96,512]{1,0:T(8,128)(2,1)S(1)}, u32[]{:S(2)}, u32[]{:S(2)}) collective-permute-start(bf16[96,512]{1,0:T(8,128)(2,1)S(1)} %collective-permute-done.5), channel_id=1, source_target_pairs={{0,15},{1,0},{2,1},{3,2},{4,3},{5,4},{6,5},{7,6},{8,7},{9,8},{10,9... | collective-permute-start | bytes 294920 | tf_op jit(solution)/shard_map/ppermute | solution.py:146
  204.0 6.7 %collective-permute-start.8 = (bf16[96,512]{1,0:T(8,128)(2,1)S(1)}, bf16[96,512]{1,0:T(8,128)(2,1)S(1)}, u32[]{:S(2)}, u32[]{:S(2)}) collective-permute-start(bf16[96,512]{1,0:T(8,128)(2,1)S(1)} %collective-permute-done.6), channel_id=1, source_target_pairs={{0,1},{1,2},{2,3},{3,4},{4,5},{5,6},{6,7},{7,8},{8,9},{9,10},{10,1... | collective-permute-start | bytes 294920 | tf_op jit(solution)/shard_map/ppermute | solution.py:139
  204.0 6.8 %collective-permute-start.9 = (bf16[96,512]{1,0:T(8,128)(2,1)S(1)}, bf16[96,512]{1,0:T(8,128)(2,1)S(1)}, u32[]{:S(2)}, u32[]{:S(2)}) collective-permute-start(bf16[96,512]{1,0:T(8,128)(2,1)S(1)} %collective-permute-done.7), channel_id=1, source_target_pairs={{0,15},{1,0},{2,1},{3,2},{4,3},{5,4},{6,5},{7,6},{8,7},{9,8},{10,9... | collective-permute-start | bytes 294920 | tf_op jit(solution)/shard_map/ppermute | solution.py:146
  210.7 6.8 %collective-permute-start.10 = (bf16[96,512]{1,0:T(8,128)(2,1)S(1)}, bf16[96,512]{1,0:T(8,128)(2,1)S(1)}, u32[]{:S(2)}, u32[]{:S(2)}) collective-permute-start(bf16[96,512]{1,0:T(8,128)(2,1)S(1)} %collective-permute-done.8), channel_id=1, source_target_pairs={{0,1},{1,2},{2,3},{3,4},{4,5},{5,6},{6,7},{7,8},{8,9},{9,10},{10,1... | collective-permute-start | bytes 294920 | tf_op jit(solution)/shard_map/ppermute | solution.py:139
  210.7 6.8 %collective-permute-start.11 = (bf16[96,512]{1,0:T(8,128)(2,1)S(1)}, bf16[96,512]{1,0:T(8,128)(2,1)S(1)}, u32[]{:S(2)}, u32[]{:S(2)}) collective-permute-start(bf16[96,512]{1,0:T(8,128)(2,1)S(1)} %collective-permute-done.9), channel_id=1, source_target_pairs={{0,15},{1,0},{2,1},{3,2},{4,3},{5,4},{6,5},{7,6},{8,7},{9,8},{10,9... | collective-permute-start | bytes 294920 | tf_op jit(solution)/shard_map/ppermute | solution.py:146
  217.5 6.7 %collective-permute-start.12 = (bf16[96,512]{1,0:T(8,128)(2,1)S(1)}, bf16[96,512]{1,0:T(8,128)(2,1)S(1)}, u32[]{:S(2)}, u32[]{:S(2)}) collective-permute-start(bf16[96,512]{1,0:T(8,128)(2,1)S(1)} %collective-permute-done.10), channel_id=1, source_target_pairs={{0,1},{1,2},{2,3},{3,4},{4,5},{5,6},{6,7},{7,8},{8,9},{9,10},{10,1... | collective-permute-start | bytes 294920 | tf_op jit(solution)/shard_map/ppermute | solution.py:139
  217.6 6.8 %collective-permute-start.13 = (bf16[96,512]{1,0:T(8,128)(2,1)S(1)}, bf16[96,512]{1,0:T(8,128)(2,1)S(1)}, u32[]{:S(2)}, u32[]{:S(2)}) collective-permute-start(bf16[96,512]{1,0:T(8,128)(2,1)S(1)} %collective-permute-done.11), channel_id=1, source_target_pairs={{0,15},{1,0},{2,1},{3,2},{4,3},{5,4},{6,5},{7,6},{8,7},{9,8},{10,9... | collective-permute-start | bytes 294920 | tf_op jit(solution)/shard_map/ppermute | solution.py:146
  224.2 6.7 %collective-permute-start.14 = (bf16[96,512]{1,0:T(8,128)(2,1)S(1)}, bf16[96,512]{1,0:T(8,128)(2,1)S(1)}, u32[]{:S(2)}, u32[]{:S(2)}) collective-permute-start(bf16[96,512]{1,0:T(8,128)(2,1)S(1)} %collective-permute-done.12), channel_id=1, source_target_pairs={{0,1},{1,2},{2,3},{3,4},{4,5},{5,6},{6,7},{7,8},{8,9},{9,10},{10,1... | collective-permute-start | bytes 294920 | tf_op jit(solution)/shard_map/ppermute | solution.py:139
  231.6 1.3 copy-start.10
  234.1 1.1 copy-start.1
  240.7 3.1 %copy-start.7 = (bf16[96,16,256]{2,0,1:T(8,128)(2,1)S(1)}, bf16[96,16,256]{2,0,1:T(8,128)(2,1)}, u32[]{:S(2)}) copy-start(bf16[96,16,256]{2,0,1:T(8,128)(2,1)} %copy-done.6) | copy-start | bytes 2359300
  240.7 3.1 %copy-start.15 = (bf16[1536,256]{0,1:T(8,128)(2,1)S(1)}, bf16[1536,256]{0,1:T(8,128)(2,1)}, u32[]{:S(2)}) copy-start(bf16[1536,256]{0,1:T(8,128)(2,1)} %copy-done.14) | copy-start | bytes 2359300
  240.9 18.5 %collective-permute-start.16 = (bf16[1536,2]{1,0:T(8,128)(2,1)S(1)}, bf16[1536,2]{1,0:T(8,128)(2,1)S(1)}, u32[]{:S(2)}, u32[]{:S(2)}) collective-permute-start(bf16[1536,2]{1,0:T(8,128)(2,1)S(1)} %get-tuple-element.9), channel_id=1, source_target_pairs={{0,16},{1,17},{2,18},{3,19},{4,20},{5,21},{6,22},{7,23},{8,24},{9,... | collective-permute-start | bytes 18440 | tf_op jit(solution)/shard_map/ppermute | solution.py:15
  247.4 16.9 %collective-permute-start.15 = (bf16[1536,2]{1,0:T(8,128)(2,1)S(1)}, bf16[1536,2]{1,0:T(8,128)(2,1)}, u32[]{:S(2)}, u32[]{:S(2)}) collective-permute-start(bf16[1536,2]{1,0:T(8,128)(2,1)S(1)} %get-tuple-element.8), channel_id=1, source_target_pairs={{16,0},{17,1},{18,2},{19,3},{20,4},{21,5},{22,6},{23,7},{24,8},{25... | collective-permute-start | bytes 18440 | tf_op jit(solution)/shard_map/ppermute | solution.py:17
  248.7 12.4 %copy-start.12 = (bf16[5,96,1536]{2,1,0:T(8,128)(2,1)S(1)}, bf16[5,96,1536]{2,1,0:T(8,128)(2,1)}, u32[]{:S(2)}) copy-start(bf16[5,96,1536]{2,1,0:T(8,128)(2,1)} %all-gather.2.cloned.1.call-done) | copy-start | bytes 4423684
  266.1 1.8 copy-start.3
Sparse Core Ops, SparseCore 0:
  145.5 26.4 reduce-scatter.2
  173.6 26.3 all-gather.1
  235.4 28.5 reduce-scatter.4
